TPU v7x, 32 devices: a whole 2x2x4 slice. The times are simulated.
32 devices in a mesh: parts: 2 (over y), track: 4 (over z), tm: 2 (over x), coef: 2 (over core).
Axes of the slice: x: 2, y: 2, z: 4, core: 2. Of those that a mesh axis runs over, the one named last changes fastest.
Arguments:
- sector_ids: int32 [12288], P(('parts', 'track', 'tm')), parts along dimension 0, may hold values from 0 to 63, as said below
- observed: float32 [3, 12288], P(None, ('parts', 'track', 'tm')), parts along dimension 1, may hold values from -6 to 6
- weights: float32 [3, 12288], P(None, ('parts', 'track', 'tm')), parts along dimension 1, may hold values from 0.3 to 3
- coefficients: float32 [2048, 128], P(('parts', 'track')), parts along dimension 0, may hold values from -6 to 6
- tile_index: int32 [128, 12], P(('parts', 'track', 'tm'), 'coef'), parts along dimension 0, may hold values from 0 to 1023, as said below
- tile_count: int32 [128], P(('parts', 'track', 'tm')), parts along dimension 0, may hold values from 3 to 12
- sensitivity: bfloat16 [128, 12, 3, 128, 128], P(('parts', 'track', 'tm'), 'coef'), parts along dimension 0, may hold values from -0.15625 to 0.15625
Outputs:
- gradient: float32 [2048, 128], P(('parts', 'track')), parts along dimension 0
There are 2 independent parts, one for each index of `parts`. A program takes and returns all parts, laid end to end along the dimension named above; each array names one. Nothing has to cross between parts.
Inputs may be any that keep to these rules, and one draw needn't show every extreme that they name: `sector_ids`: the rows of one index of track and tm fall in at most 192 rows into the 8 consecutive sectors of any one index, and some pair reaches 192; the sectors of each index receive exactly 768 rows in all; each sector holds at most 128 rows, and every index holds a sector with exactly 128. `tile_index`: entries at positions from tile_count on are arbitrary blocks and take no part. Block n belongs to track index n // 256. Of the 48 entries held by one index of track, tm and coef (its sectors' rows, its coef share of the columns), live or not, at most 24 name blocks of any one track index, and every such device has a track index named exactly 24 times.
All inputs are finite; a program needn't handle non-finite values.
Results may differ from a plain program's by a relative error of at most 0.0037.
Values may be sent and summed in bfloat16 or wider, within the bound.
A program may use at most 64 MiB of HBM per device.

v0:
```python
import jax
import jax.numpy as jnp
from jax import lax
from jax.sharding import PartitionSpec as P

HUBER = 2.0


def per_device(sector_ids, observed, weights, coefficients, tile_index, tile_count, sensitivity):
    sector_total = tile_index.shape[0]
    half_k = tile_index.shape[1]
    slot_count = sensitivity.shape[3]
    block_width = sensitivity.shape[4]
    owners = lax.axis_size(("track", "tm"))
    row_total = sector_ids.shape[0]
    capacity = 2 * row_total // owners
    rounded = coefficients.astype(jnp.bfloat16)
    every_block = lax.all_gather(rounded, "track", axis=0, tiled=True)
    owner_of = sector_ids // sector_total
    local_sector = sector_ids % sector_total
    onehot = (owner_of[:, None] == jnp.arange(owners, dtype=jnp.int32)[None, :]).astype(jnp.int32)
    ranking = jnp.sum((jnp.cumsum(onehot, axis=0) - 1) * onehot, axis=1)
    placing = owner_of * capacity + ranking
    payload = jnp.concatenate([observed, weights], axis=0)
    outgoing = jnp.zeros((6, owners * capacity), jnp.float32).at[:, placing].set(payload)
    outgoing = jnp.transpose(outgoing.reshape(6, owners, capacity), (1, 0, 2))
    labels = jnp.full((owners * capacity,), -1, jnp.int32).at[placing].set(local_sector)
    labels = labels.reshape(owners, capacity)
    got_rows, got_labels = (
        lax.all_to_all(outgoing, ("track", "tm"), split_axis=0, concat_axis=0, tiled=True),
        lax.all_to_all(labels, ("track", "tm"), split_axis=0, concat_axis=0, tiled=True),
    )
    received = jnp.transpose(got_rows, (1, 0, 2)).reshape(6, owners * capacity)
    flat_labels = got_labels.reshape(owners * capacity)
    member = (flat_labels[:, None] == jnp.arange(sector_total, dtype=jnp.int32)[None, :]).astype(
        jnp.int32
    )
    within = jnp.sum((jnp.cumsum(member, axis=0) - 1) * member, axis=1)
    target = jnp.where(
        flat_labels >= 0, flat_labels * slot_count + within, sector_total * slot_count
    )
    gridded = jnp.zeros((6, sector_total * slot_count + 1), jnp.float32).at[:, target].set(received)
    gridded = jnp.transpose(gridded[:, :-1].reshape(6, sector_total, slot_count), (1, 0, 2))
    observed_tiles = gridded[:, :3]
    weight_tiles = gridded[:, 3:]
    k_global = lax.axis_index("coef") * half_k + jnp.arange(half_k, dtype=jnp.int32)
    active = k_global[None, :] < tile_count[:, None]
    blocks = jnp.take(every_block, tile_index, axis=0)
    blocks = jnp.where(active[:, :, None], blocks, jnp.zeros_like(blocks))
    partial_pred = jnp.einsum(
        "skcjb,skb->scj", sensitivity, blocks, preferred_element_type=jnp.float32
    )
    predicted = lax.psum(partial_pred, "coef")
    scaled = weight_tiles * (predicted - observed_tiles)
    force = (weight_tiles * scaled / jnp.sqrt(1.0 + (scaled / HUBER) ** 2)).astype(jnp.bfloat16)
    tile_grad = jnp.einsum("skcjb,scj->skb", sensitivity, force, preferred_element_type=jnp.float32)
    tile_grad = jnp.where(active[:, :, None], tile_grad, jnp.zeros_like(tile_grad))
    block_total = every_block.shape[0]
    partial_grad = jnp.zeros((block_total, block_width), jnp.float32)
    partial_grad = partial_grad.at[tile_index.reshape(-1)].add(tile_grad.reshape(-1, block_width))
    summed = lax.psum_scatter(partial_grad, "track", scatter_dimension=0, tiled=True)
    gradient = lax.psum(summed, ("tm", "coef"))
    return gradient


def solution(mesh):
    placed = (
        P(("parts", "track", "tm")),
        P(None, ("parts", "track", "tm")),
        P(None, ("parts", "track", "tm")),
        P(("parts", "track"), None),
        P(("parts", "track", "tm"), "coef"),
        P(("parts", "track", "tm")),
        P(("parts", "track", "tm"), "coef", None, None, None),
    )
    return jax.shard_map(
        per_device,
        mesh=mesh,
        in_specs=placed,
        out_specs=P(("parts", "track"), None),
        check_vma=False,
    )
```

profile of v0, /device:TPU:0, one launch (start us, length us, event | category | flops | bytes accessed | tf_op | source)
XLA Modules:
  0.0 135.0 jit_solution(9949122944024813271)
XLA Ops:
  6.5 0.7 add_select_fusion
  7.2 1.7 %reduce-window.14 = s32[8,6,128]{2,0,1:T(8,128)S(1)} reduce-window(s32[8,6,128]{2,0,1:T(8,128)S(1)} %fusion.13, s32[]{:T(128)} %constant.40.clone.1), window={size=1x1x128 pad=0_0x0_0x127_0}, to_apply=%region_0.1 | reduce-window | flops 780288 | bytes 49156 | tf_op jit(solution)/shard_map/reduce-window
  8.9 0.1 slice.30
  9.0 0.1 copy.24
  9.2 0.2 reduce-window.15
  9.3 0.1 copy.25
  9.4 0.1 fusion.11
  9.5 3.4 %scatter_custom_fusion = s32[1536]{0:T(1024)S(1)} fusion(s32[768]{0:T(1024)S(1)} %compare_select_fusion.2, s32[768]{0:T(1024)S(1)} %get-tuple-element.7, s32[]{:T(128)} %constant.74.clone.1), kind=kCustom, calls=%fused_computation.50 | custom fusion | bytes 6148 | tf_op jit(solution)/shard_map/scatter | solution.py:27
  12.9 0.7 all_to_all.9
  13.6 7.3 %all-to-all-start = ((s32[8,1,192]{2,1,0:T(1,128)}), s32[8,1,192]{2,1,0:T(1,128)S(1)}, u32[]{:S(2)}, u32[]{:S(2)}) async-start(s32[8,1,192]{2,1,0:T(1,128)} %all_to_all.9), calls=%async_computation | async-start | bytes 16384 | tf_op jit(solution)/shard_map/all_to_all | solution.py:31
  20.8 0.7 compare_select_fusion.1
  21.5 0.8 reshape.166
  22.3 0.7 maximum_bitcast_fusion
  23.0 0.2 copy.26
  23.2 4.4 %scatter_custom_fusion.1 = f32[6,1536]{0,1:T(8,128)S(1)} fusion(s32[768]{0:T(1024)S(1)} %compare_select_fusion.2, f32[768,6]{1,0:T(8,128)S(1)} %copy.26, f32[]{:T(128)} %constant.39.clone.1), kind=kCustom, calls=%fused_computation.7 | custom fusion | bytes 36868 | tf_op jit(solution)/shard_map/scatter | solution.py:25
  27.6 1.0 copy.27
  28.6 0.9 convert_element_type.18
  29.5 14.5 %all_gather.3 = bf16[1024,128]{1,0:T(8,128)(2,1)S(1)} all-gather(bf16[256,128]{1,0:T(8,128)(2,1)S(1)} %convert_element_type.18), channel_id=1, replica_groups=mesh['parts'=2,'track'=4,'tm'=2,'coef'=2] {'track'}, dimensions={0}, use_global_device_ids=true | all-gather | bytes 327680 | tf_op jit(solution)/shard_map/all_gather | solution.py:18
  44.0 0.1 reshape.175
  44.0 0.6 gather_fusion
  44.7 0.8 compare_and_fusion
  45.4 0.1 select_bitcast_fusion
  45.5 3.7 %fusion = f32[8,1,3,128,1]{3,1,4,2,0:T(1,128)S(1)} fusion(bf16[8,6,3,128,128]{4,3,2,1,0:T(8,128)(2,1)} %param.13, bf16[8,6,128,1,1]{2,1,0,3,4:T(8,128)(2,1)S(1)} %select_bitcast_fusion), kind=kOutput, calls=%fused_computation.5 | convolution fusion | flops 4718592 | bytes 4743168 | tf_op jit(solution)/shard_map/skcjb,skb->scj/dot_general | solution.py:50
  49.2 3.3 %psum.14 = f32[8,3,128]{2,0,1:T(8,128)S(1)} all-reduce(f32[8,3,128]{2,0,1:T(8,128)S(1)} %bitcast.50), channel_id=1, replica_groups=mesh['parts'=2,'track'=4,'tm'=2,'coef'=2] {'coef'}, use_global_device_ids=true, to_apply=%region_9.10 | all-reduce | flops 3072 | bytes 24576 | tf_op jit(solution)/shard_map/psum | solution.py:53
  52.5 0.0 all-to-all-done
  52.5 5.7 %all-to-all-start.1 = ((f32[8,6,192]{2,1,0:T(8,128)}), f32[8,6,192]{2,1,0:T(8,128)S(1)}, u32[]{:S(2)}, u32[]{:S(2)}) async-start(f32[8,6,192]{2,1,0:T(8,128)} %bitcast.8), calls=%async_computation.1 | async-start | bytes 131072 | tf_op jit(solution)/shard_map/all_to_all | solution.py:30
  58.2 0.0 reduce-scatter.2.cloned.1.call-start
  58.3 0.1 eq.61
  58.4 0.1 eq.57
  58.5 2.3 %reduce-window.16 = s32[8,12,128]{2,1,0:T(8,128)S(1)} reduce-window(s32[8,12,128]{2,1,0:T(8,128)S(1)} %fusion.8, s32[]{:T(128)} %constant.40.clone.1), window={size=1x1x128 pad=0_0x0_0x127_0}, to_apply=%region_4.5 | reduce-window | flops 1560576 | bytes 98308 | tf_op jit(solution)/shard_map/reduce-window.2
  60.7 0.3 slice_reduce_fusion
  61.0 0.2 reduce-window.19
  61.2 0.1 add_bitcast_fusion
  61.3 0.1 mul.43
  61.4 0.1 ge.21
  61.6 3.5 %all-to-all-done.1 = f32[8,6,192]{2,1,0:T(8,128)S(1)} async-done(((f32[8,6,192]{2,1,0:T(8,128)}), f32[8,6,192]{2,1,0:T(8,128)S(1)}, u32[]{:S(2)}, u32[]{:S(2)}) %all-to-all-start.1) | async-done | bytes 36896 | tf_op jit(solution)/shard_map/all_to_all | solution.py:30
  65.1 0.1 reshape.198
  65.2 0.3 copy.29
  65.5 4.4 %scatter_custom_fusion.2 = f32[6,1025]{0,1:T(8,128)S(1)} fusion(s32[1536]{0:T(1024)S(1)} %fusion.17, f32[1536,6]{1,0:T(8,128)S(1)} %copy.29, f32[]{:T(128)} %constant.39.clone.1), kind=kCustom, calls=%fused_computation.9 | custom fusion | bytes 24604 | tf_op jit(solution)/shard_map/scatter | solution.py:42
  70.0 0.2 copy.36
  70.2 3.1 %fusion.15 = f32[8,1,6,128,1]{3,1,4,2,0:T(1,128)S(1)} fusion(bf16[8,6,3,128,128]{4,3,2,1,0:T(8,128)(2,1)} %param.13, bf16[8,3,128,1,1]{2,0,1,3,4:T(8,128)(2,1)S(1)} %fusion.18), kind=kOutput, calls=%fused_computation.34 | convolution fusion | flops 4718592 | bytes 4749312 | tf_op jit(solution)/shard_map/skcjb,scj->skb/dot_general | solution.py:56
  73.3 0.1 bitcast_select_fusion
  73.4 1.5 %scatter_custom_fusion.3 = f32[1024,128]{1,0:T(8,128)} fusion(s32[48]{0:T(128)S(1)} %fusion.23, f32[48,128]{1,0:T(8,128)S(1)} %reshape.209, f32[]{:T(128)} %constant.39.clone.1), kind=kCustom, calls=%fused_computation.11 | custom fusion | flops 6144 | bytes 524292 | tf_op jit(solution)/shard_map/scatter-add | solution.py:60
  74.9 0.0 reduce-scatter.2.cloned.1.call-update
  75.0 0.0 all-reduce.2.cloned.1.call-start
  75.0 19.6 %reduce-scatter.2.cloned.1.call-done = f32[256,128]{1,0:T(8,128)} async-done(((f32[1024,128]{1,0:T(8,128)}), f32[256,128]{1,0:T(8,128)}) %reduce-scatter.2.cloned.1.call-update) | async-done | bytes 131088 | tf_op jit(solution)/shard_map/reduce_scatter | solution.py:61
  94.6 0.0 all-reduce.2.cloned.1.call-update
  94.7 32.0 %all-reduce.2.cloned.1.call-done = f32[256,128]{1,0:T(8,128)} async-done(((f32[256,128]{1,0:T(8,128)}), f32[256,128]{1,0:T(8,128)}) %all-reduce.2.cloned.1.call-update) | async-done | bytes 131088 | tf_op jit(solution)/shard_map/psum | solution.py:62
  126.6 1.6 %copy.49 = f32[256,128]{1,0:T(8,128)} copy(f32[256,128]{1,0:T(8,128)} %all-reduce.2.cloned.1.call-done) | data formatting | bytes 262144
  (16 shorter events, 0.3 us)
Async XLA Ops:
  13.6 38.9 %all-to-all-start = ((s32[8,1,192]{2,1,0:T(1,128)}), s32[8,1,192]{2,1,0:T(1,128)S(1)}, u32[]{:S(2)}, u32[]{:S(2)}) async-start(s32[8,1,192]{2,1,0:T(1,128)} %all_to_all.9), calls=%async_computation | async-start | bytes 16384 | tf_op jit(solution)/shard_map/all_to_all | solution.py:31
  52.5 12.6 %all-to-all-start.1 = ((f32[8,6,192]{2,1,0:T(8,128)}), f32[8,6,192]{2,1,0:T(8,128)S(1)}, u32[]{:S(2)}, u32[]{:S(2)}) async-start(f32[8,6,192]{2,1,0:T(8,128)} %bitcast.8), calls=%async_computation.1 | async-start | bytes 131072 | tf_op jit(solution)/shard_map/all_to_all | solution.py:30
  58.2 36.4 %reduce-scatter.2.cloned.1.call-start = ((), (), s32[]{:S(2)}) async-start(), calls=%async_computation.3 | async-start | bytes 655360 | tf_op jit(solution)/shard_map/reduce_scatter | solution.py:61
  75.0 51.7 %all-reduce.2.cloned.1.call-start = ((), (), s32[]{:S(2)}) async-start(), calls=%async_computation.4 | async-start | bytes 262144 | tf_op jit(solution)/shard_map/psum | solution.py:62
Sparse Core Ops, SparseCore 0:
  75.1 19.5 reduce-scatter.1
  97.0 29.6 all-reduce.1
where the time goes:
time: 136 us; the launch traced here: 135 us
  waiting for transfers between devices  55.2 us (41%)
  local copies, waits for them, and re-layouts  18.6 us (14%)
  blocking collectives  17.8 us (13%)
  between operations  13.5 us (10%)
  starting transfers between devices  13.1 us (10%)
  other arithmetic  10.2 us (7%)
  matrix products  6.73 us (5%)
    psum x1, waiting for transfers between devices, per_device(): gradient = lax.psum(summed, ('tm', 'coef'))  32 us
    reduce_scatter x1, waiting for transfers between devices, per_device(): lax.psum_scatter(partial_grad, 'track', scatter_dimension=0, tiled=True)  19.6 us
    all_gather x1, blocking collectives, per_device(): every_block = lax.all_gather(rounded, 'track', axis=0, tiled=True)  14.5 us
    all_to_all x1, starting transfers between devices, per_device(): lax.all_to_all(labels, ('track', 'tm'), split_axis=0, concat_axis=0, tile...  7.25 us
    all_to_all x1, starting transfers between devices, per_device(): lax.all_to_all(outgoing, ('track', 'tm'), split_axis=0, concat_axis=0, ti...  5.72 us
    scatter x1, local copies, waits for them, and re-layouts, per_device(): jnp.zeros((6, sector_total * slot_count + 1), jnp.float32).at[:, target]  4.45 us
    scatter x1, local copies, waits for them, and re-layouts, per_device(): jnp.zeros((6, owners * capacity), jnp.float32).at[:, placing].set(payload)  4.36 us
    another operation x4, other arithmetic  4.31 us
  transfers between devices with their start and end apart: 4, of which 3 were waited for; matrix products, arithmetic and copies ran while one was open for 13% of the time, Pallas kernels for 0%

commit v1 on v0

--- a/solution.py
+++ b/solution.py
@@ -4,6 +4,12 @@
 from jax.sharding import PartitionSpec as P
 
 HUBER = 2.0
+
+
+def in_order(pieces, dim):
+    dims = list(pieces.shape[1:])
+    dims[dim] *= pieces.shape[0]
+    return jnp.moveaxis(pieces, 0, dim).reshape(dims)
 
 
 def per_device(sector_ids, observed, weights, coefficients, tile_index, tile_count, sensitivity):
@@ -15,7 +21,19 @@
     row_total = sector_ids.shape[0]
     capacity = 2 * row_total // owners
     rounded = coefficients.astype(jnp.bfloat16)
-    every_block = lax.all_gather(rounded, "track", axis=0, tiled=True)
+    devices = lax.axis_size("track")
+    pairs = [(i, (i + 1) % devices) for i in range(devices)]
+    back = [(b, a) for a, b in pairs]
+    lower, upper = ([], [])
+    for step in range(devices - 1):
+        if step % 2 == 0:
+            lower.append(lax.ppermute(lower[-1] if lower else rounded, "track", pairs))
+        else:
+            upper.append(lax.ppermute(upper[-1] if upper else rounded, "track", back))
+    pieces = jnp.stack([*lower[::-1], rounded, *upper])
+    shift = lax.axis_index("track") - len(lower)
+    pieces = pieces[(jnp.arange(devices) - shift) % devices]
+    every_block = in_order(pieces, 0)
     owner_of = sector_ids // sector_total
     local_sector = sector_ids % sector_total
     onehot = (owner_of[:, None] == jnp.arange(owners, dtype=jnp.int32)[None, :]).astype(jnp.int32)

time: 136 us -> 126 us (0.926)
  blocking collectives: 17.8 us -> 3.3 us
  starting transfers between devices: 13.1 us -> 17.4 us
  waiting for transfers between devices: 55.2 us -> 53.8 us
    all_gather x1 -> x0, blocking collectives: 14.5 us -> none  [per_device(): every_block = lax.all_gather(rounded, 'track', axis=0, tiled=True)]
    ppermute x0 -> x3, starting transfers between devices: none -> 7.14 us  [the longest x2 5.05 us: per_device(): lower.append(lax.ppermute(lower[-1] if lower else rounded, 'track', pairs))]
    all_to_all x1, starting transfers between devices: 7.25 us -> 4.17 us  [per_device(): lax.all_to_all(labels, ('track', 'tm'), split_axis=0, concat_axis=0, tile...]
    all_to_all x1, waiting for transfers between devices: 3.54 us -> 1.51 us  [per_device(): lax.all_to_all(outgoing, ('track', 'tm'), split_axis=0, concat_axis=0, ti...]
    another operation x4 -> x6, other arithmetic: 4.31 us -> 5.26 us
  transfers between devices with their start and end apart: 4 -> 7, of which waited for: 3 -> 3; matrix products, arithmetic and copies ran while one was open for 13% -> 19% of each run, Pallas kernels for 0% -> 0%
where the time goes in v1:
time: 126 us; the launch traced here: 125 us
  waiting for transfers between devices  53.8 us (43%)
  local copies, waits for them, and re-layouts  19.2 us (15%)
  starting transfers between devices  17.4 us (14%)
  between operations  13.6 us (11%)
  other arithmetic  11.1 us (9%)
  matrix products  6.73 us (5%)
  blocking collectives  3.3 us (3%)
    psum x1, waiting for transfers between devices, per_device(): gradient = lax.psum(summed, ('tm', 'coef'))  31.9 us
    reduce_scatter x1, waiting for transfers between devices, per_device(): lax.psum_scatter(partial_grad, 'track', scatter_dimension=0, tiled=True)  20.3 us
    all_to_all x1, starting transfers between devices, per_device(): lax.all_to_all(outgoing, ('track', 'tm'), split_axis=0, concat_axis=0, ti...  6 us
    ppermute x2, starting transfers between devices, per_device(): lower.append(lax.ppermute(lower[-1] if lower else rounded, 'track', pairs))  5.05 us
    scatter x1, local copies, waits for them, and re-layouts, per_device(): jnp.zeros((6, sector_total * slot_count + 1), jnp.float32).at[:, target]  4.45 us
    scatter x1, local copies, waits for them, and re-layouts, per_device(): jnp.zeros((6, owners * capacity), jnp.float32).at[:, placing].set(payload)  4.36 us
    another operation x4, other arithmetic  4.31 us
    all_to_all x1, starting transfers between devices, per_device(): lax.all_to_all(labels, ('track', 'tm'), split_axis=0, concat_axis=0, tile...  4.17 us
  transfers between devices with their start and end apart: 7, of which 3 were waited for; matrix products, arithmetic and copies ran while one was open for 19% of the time, Pallas kernels for 0%

profile of v1, /device:TPU:0, one launch (start us, length us, event | category | flops | bytes accessed | tf_op | source)
XLA Modules:
  0.0 125.1 jit_solution(17426266086211105092)
XLA Ops:
  6.5 0.9 convert_element_type.18
  7.4 3.0 %collective-permute-start = (bf16[256,128]{1,0:T(8,128)(2,1)S(1)}, bf16[256,128]{1,0:T(8,128)(2,1)S(1)}, u32[]{:S(2)}, u32[]{:S(2)}) collective-permute-start(bf16[256,128]{1,0:T(8,128)(2,1)S(1)} %convert_element_type.18), channel_id=1, source_target_pairs={{0,4},{4,8},{8,12},{12,0},{1,5},{5,9},{9,13},{13,1},{2,6},{6,10},{... | collective-permute-start | bytes 196616 | tf_op jit(solution)/shard_map/ppermute | solution.py:30
  10.5 2.1 %collective-permute-start.2 = (bf16[256,128]{1,0:T(8,128)(2,1)S(1)}, bf16[256,128]{1,0:T(8,128)(2,1)S(1)}, u32[]{:S(2)}, u32[]{:S(2)}) collective-permute-start(bf16[256,128]{1,0:T(8,128)(2,1)S(1)} %convert_element_type.18), channel_id=1, source_target_pairs={{4,0},{8,4},{12,8},{0,12},{5,1},{9,5},{13,9},{1,13},{6,2},{10,6},{... | collective-permute-start | bytes 196616 | tf_op jit(solution)/shard_map/ppermute | solution.py:32
  12.6 0.7 add_select_fusion
  13.3 1.7 %reduce-window.14 = s32[8,6,128]{2,0,1:T(8,128)S(1)} reduce-window(s32[8,6,128]{2,0,1:T(8,128)S(1)} %fusion.13, s32[]{:T(128)} %constant.54.clone.1), window={size=1x1x128 pad=0_0x0_0x127_0}, to_apply=%region_0.1 | reduce-window | flops 780288 | bytes 49156 | tf_op jit(solution)/shard_map/reduce-window
  15.0 0.1 slice.32
  15.0 0.1 copy.24
  15.2 0.2 reduce-window.15
  15.3 0.1 copy.25
  15.4 0.1 fusion.11
  15.5 3.4 %scatter_custom_fusion = s32[1536]{0:T(1024)S(1)} fusion(s32[768]{0:T(1024)S(1)} %compare_select_fusion.2, s32[768]{0:T(1024)S(1)} %get-tuple-element.7, s32[]{:T(128)} %constant.93.clone.1), kind=kCustom, calls=%fused_computation.53 | custom fusion | bytes 6148 | tf_op jit(solution)/shard_map/scatter | solution.py:45
  18.9 0.7 all_to_all.9
  19.6 4.2 %all-to-all-start = ((s32[8,1,192]{2,1,0:T(1,128)}), s32[8,1,192]{2,1,0:T(1,128)S(1)}, u32[]{:S(2)}, u32[]{:S(2)}) async-start(s32[8,1,192]{2,1,0:T(1,128)} %all_to_all.9), calls=%async_computation | async-start | bytes 16384 | tf_op jit(solution)/shard_map/all_to_all | solution.py:49
  23.8 0.9 convert_bitcast_fusion
  24.7 0.7 compare_select_fusion.1
  25.4 0.8 reshape.218
  26.2 0.1 reshape.236
  26.3 0.7 maximum_bitcast_fusion
  27.0 0.8 compare_and_fusion
  27.8 0.2 copy.26
  28.0 4.4 %scatter_custom_fusion.1 = f32[6,1536]{0,1:T(8,128)S(1)} fusion(s32[768]{0:T(1024)S(1)} %compare_select_fusion.2, f32[768,6]{1,0:T(8,128)S(1)} %copy.26, f32[]{:T(128)} %constant.53.clone.1), kind=kCustom, calls=%fused_computation.8 | custom fusion | bytes 36868 | tf_op jit(solution)/shard_map/scatter | solution.py:43
  32.3 1.0 copy.27
  33.3 0.0 all-to-all-done
  33.3 6.0 %all-to-all-start.1 = ((f32[8,6,192]{2,1,0:T(8,128)}), f32[8,6,192]{2,1,0:T(8,128)S(1)}, u32[]{:S(2)}, u32[]{:S(2)}) async-start(f32[8,6,192]{2,1,0:T(8,128)} %bitcast.8), calls=%async_computation.1 | async-start | bytes 131072 | tf_op jit(solution)/shard_map/all_to_all | solution.py:48
  39.3 0.0 reduce-scatter.2.cloned.1.call-start
  39.4 0.1 eq.63
  39.5 0.1 eq.59
  39.5 2.3 %reduce-window.16 = s32[8,12,128]{2,1,0:T(8,128)S(1)} reduce-window(s32[8,12,128]{2,1,0:T(8,128)S(1)} %fusion.8, s32[]{:T(128)} %constant.54.clone.1), window={size=1x1x128 pad=0_0x0_0x127_0}, to_apply=%region_4.5 | reduce-window | flops 1560576 | bytes 98308 | tf_op jit(solution)/shard_map/reduce-window.2
  41.8 0.3 slice_reduce_fusion
  42.1 0.2 reduce-window.19
  42.3 0.1 add_bitcast_fusion
  42.4 0.1 mul.43
  42.5 0.1 ge.21
  42.6 0.0 collective-permute-done
  42.6 2.0 %collective-permute-start.1 = (bf16[256,128]{1,0:T(8,128)(2,1)S(1)}, bf16[256,128]{1,0:T(8,128)(2,1)S(1)}, u32[]{:S(2)}, u32[]{:S(2)}) collective-permute-start(bf16[256,128]{1,0:T(8,128)(2,1)S(1)} %collective-permute-done), channel_id=1, source_target_pairs={{0,4},{4,8},{8,12},{12,0},{1,5},{5,9},{9,13},{13,1},{2,6},{6,10},{... | collective-permute-start | bytes 196616 | tf_op jit(solution)/shard_map/ppermute | solution.py:30
  44.7 1.5 %all-to-all-done.1 = f32[8,6,192]{2,1,0:T(8,128)S(1)} async-done(((f32[8,6,192]{2,1,0:T(8,128)}), f32[8,6,192]{2,1,0:T(8,128)S(1)}, u32[]{:S(2)}, u32[]{:S(2)}) %all-to-all-start.1) | async-done | bytes 36896 | tf_op jit(solution)/shard_map/all_to_all | solution.py:48
  46.2 0.1 reshape.259
  46.3 0.3 copy.29
  46.6 4.4 %scatter_custom_fusion.2 = f32[6,1025]{0,1:T(8,128)S(1)} fusion(s32[1536]{0:T(1024)S(1)} %fusion.17, f32[1536,6]{1,0:T(8,128)S(1)} %copy.29, f32[]{:T(128)} %constant.53.clone.1), kind=kCustom, calls=%fused_computation.10 | custom fusion | bytes 24604 | tf_op jit(solution)/shard_map/scatter | solution.py:60
  51.1 0.2 copy.36
  51.3 0.0 collective-permute-done.2
  51.3 0.0 collective-permute-done.1
  51.4 0.6 gather_fusion
  52.0 0.6 gather_fusion.1
  52.6 0.1 select_bitcast_fusion
  52.7 3.7 %fusion = f32[8,1,3,128,1]{3,1,4,2,0:T(1,128)S(1)} fusion(bf16[8,6,3,128,128]{4,3,2,1,0:T(8,128)(2,1)} %param.13, bf16[8,6,128,1,1]{2,1,0,3,4:T(8,128)(2,1)S(1)} %select_bitcast_fusion), kind=kOutput, calls=%fused_computation.6 | convolution fusion | flops 4718592 | bytes 4743168 | tf_op jit(solution)/shard_map/skcjb,skb->scj/dot_general | solution.py:68
  56.3 3.3 %psum.14 = f32[8,3,128]{2,0,1:T(8,128)S(1)} all-reduce(f32[8,3,128]{2,0,1:T(8,128)S(1)} %bitcast.62), channel_id=1, replica_groups=mesh['parts'=2,'track'=4,'tm'=2,'coef'=2] {'coef'}, use_global_device_ids=true, to_apply=%region_9.10 | all-reduce | flops 3072 | bytes 24576 | tf_op jit(solution)/shard_map/psum | solution.py:71
  59.7 3.1 %fusion.15 = f32[8,1,6,128,1]{3,1,4,2,0:T(1,128)S(1)} fusion(bf16[8,6,3,128,128]{4,3,2,1,0:T(8,128)(2,1)} %param.13, bf16[8,3,128,1,1]{2,0,1,3,4:T(8,128)(2,1)S(1)} %fusion.18), kind=kOutput, calls=%fused_computation.36 | convolution fusion | flops 4718592 | bytes 4749312 | tf_op jit(solution)/shard_map/skcjb,scj->skb/dot_general | solution.py:74
  62.7 0.1 bitcast_select_fusion
  62.8 1.5 %scatter_custom_fusion.3 = f32[1024,128]{1,0:T(8,128)} fusion(s32[48]{0:T(128)S(1)} %fusion.24, f32[48,128]{1,0:T(8,128)S(1)} %reshape.270, f32[]{:T(128)} %constant.53.clone.1), kind=kCustom, calls=%fused_computation.13 | custom fusion | flops 6144 | bytes 524292 | tf_op jit(solution)/shard_map/scatter-add | solution.py:78
  64.4 0.0 reduce-scatter.2.cloned.1.call-update
  64.4 0.0 all-reduce.2.cloned.1.call-start
  64.4 20.3 %reduce-scatter.2.cloned.1.call-done = f32[256,128]{1,0:T(8,128)} async-done(((f32[1024,128]{1,0:T(8,128)}), f32[256,128]{1,0:T(8,128)}) %reduce-scatter.2.cloned.1.call-update) | async-done | bytes 131088 | tf_op jit(solution)/shard_map/reduce_scatter | solution.py:79
  84.7 0.0 all-reduce.2.cloned.1.call-update
  84.7 31.9 %all-reduce.2.cloned.1.call-done = f32[256,128]{1,0:T(8,128)} async-done(((f32[256,128]{1,0:T(8,128)}), f32[256,128]{1,0:T(8,128)}) %all-reduce.2.cloned.1.call-update) | async-done | bytes 131088 | tf_op jit(solution)/shard_map/psum | solution.py:80
  116.7 1.6 %copy.49 = f32[256,128]{1,0:T(8,128)} copy(f32[256,128]{1,0:T(8,128)} %all-reduce.2.cloned.1.call-done) | data formatting | bytes 262144
  (19 shorter events, 0.3 us)
Async XLA Ops:
  7.4 35.2 %collective-permute-start = (bf16[256,128]{1,0:T(8,128)(2,1)S(1)}, bf16[256,128]{1,0:T(8,128)(2,1)S(1)}, u32[]{:S(2)}, u32[]{:S(2)}) collective-permute-start(bf16[256,128]{1,0:T(8,128)(2,1)S(1)} %convert_element_type.18), channel_id=1, source_target_pairs={{0,4},{4,8},{8,12},{12,0},{1,5},{5,9},{9,13},{13,1},{2,6},{6,10},{... | collective-permute-start | bytes 196616 | tf_op jit(solution)/shard_map/ppermute | solution.py:30
  10.5 40.8 %collective-permute-start.2 = (bf16[256,128]{1,0:T(8,128)(2,1)S(1)}, bf16[256,128]{1,0:T(8,128)(2,1)S(1)}, u32[]{:S(2)}, u32[]{:S(2)}) collective-permute-start(bf16[256,128]{1,0:T(8,128)(2,1)S(1)} %convert_element_type.18), channel_id=1, source_target_pairs={{4,0},{8,4},{12,8},{0,12},{5,1},{9,5},{13,9},{1,13},{6,2},{10,6},{... | collective-permute-start | bytes 196616 | tf_op jit(solution)/shard_map/ppermute | solution.py:32
  19.6 13.7 %all-to-all-start = ((s32[8,1,192]{2,1,0:T(1,128)}), s32[8,1,192]{2,1,0:T(1,128)S(1)}, u32[]{:S(2)}, u32[]{:S(2)}) async-start(s32[8,1,192]{2,1,0:T(1,128)} %all_to_all.9), calls=%async_computation | async-start | bytes 16384 | tf_op jit(solution)/shard_map/all_to_all | solution.py:49
  33.3 12.9 %all-to-all-start.1 = ((f32[8,6,192]{2,1,0:T(8,128)}), f32[8,6,192]{2,1,0:T(8,128)S(1)}, u32[]{:S(2)}, u32[]{:S(2)}) async-start(f32[8,6,192]{2,1,0:T(8,128)} %bitcast.8), calls=%async_computation.1 | async-start | bytes 131072 | tf_op jit(solution)/shard_map/all_to_all | solution.py:48
  39.3 45.4 %reduce-scatter.2.cloned.1.call-start = ((), (), s32[]{:S(2)}) async-start(), calls=%async_computation.3 | async-start | bytes 655360 | tf_op jit(solution)/shard_map/reduce_scatter | solution.py:79
  42.6 8.7 %collective-permute-start.1 = (bf16[256,128]{1,0:T(8,128)(2,1)S(1)}, bf16[256,128]{1,0:T(8,128)(2,1)S(1)}, u32[]{:S(2)}, u32[]{:S(2)}) collective-permute-start(bf16[256,128]{1,0:T(8,128)(2,1)S(1)} %collective-permute-done), channel_id=1, source_target_pairs={{0,4},{4,8},{8,12},{12,0},{1,5},{5,9},{9,13},{13,1},{2,6},{6,10},{... | collective-permute-start | bytes 196616 | tf_op jit(solution)/shard_map/ppermute | solution.py:30
  64.4 52.3 %all-reduce.2.cloned.1.call-start = ((), (), s32[]{:S(2)}) async-start(), calls=%async_computation.4 | async-start | bytes 262144 | tf_op jit(solution)/shard_map/psum | solution.py:80
Sparse Core Ops, SparseCore 0:
  64.5 20.1 reduce-scatter.1
  87.0 29.5 all-reduce.1
